TPU v7x, 256 devices: a whole 4x4x8 slice. The times are simulated.
256 devices in a mesh: seq: 64 (over x, z_lo, y), tp: 4 (over z_hi, core).
Axes of the slice: x: 4, y: 4, z: 8 (z_hi: 2, z_lo: 4; z = z_hi * 4 + z_lo), core: 2. Of those that a mesh axis runs over, the one named last changes fastest.
Arguments:
- latents: float32 [256, 256, 1152], P('tp', 'seq'), may hold values from -100 to 100
- time_embed: float32 [256, 1152], P('seq'), may hold values from -3 to 3
- modulation: float32 [3, 3, 1152], replicated, may hold values from -2 to 2
- qkv_weight: bfloat16 [2, 1152, 3, 1152], P(None, None, None, 'tp'), may hold values from -6 to 6
- out_weight: bfloat16 [2, 1152, 1152], P(None, 'tp'), may hold values from -0.1875 to 0.1875
- mlp_in_weight: bfloat16 [1152, 4608], P(None, 'tp'), may hold values from -0.1875 to 0.1875
- mlp_out_weight: bfloat16 [4608, 1152], P('tp'), may hold values from -0.09375 to 0.09375
Outputs:
- result: float32 [256, 256, 1152], P('tp', 'seq')
All inputs are finite; a program needn't handle non-finite values.
Results may differ from a plain program's by a relative error of at most 0.0045.
Values may be sent and summed in bfloat16 or wider, within the bound.
No kernel may reach another device: no remote copies, remote signals or barrier semaphores. Data moves between devices by JAX's collectives and lax.ppermute only.
A program may use at most 128 MiB of HBM per device.

v0:
```python
import math

import jax
import jax.numpy as jnp
from jax import lax
from jax.sharding import PartitionSpec as P

HD = 72


def modulate(hidden, gains):
    average = jnp.mean(hidden, axis=-1, keepdims=True)
    centred = hidden - average
    spread = jnp.mean(centred * centred, axis=-1, keepdims=True)
    return (centred * lax.rsqrt(spread + 1e-06) * (1.0 + gains[1]) + gains[0]).astype(jnp.bfloat16)


def attend(queries, key_rows, values, score_form, mix_form):
    scores = jnp.einsum(score_form, queries, key_rows, precision=lax.Precision.HIGHEST) * (
        1.0 / math.sqrt(HD)
    )
    highest = jnp.max(scores, axis=-1, keepdims=True)
    exponent = jnp.exp(scores - highest)
    weights = (exponent / jnp.sum(exponent, axis=-1, keepdims=True)).astype(jnp.bfloat16)
    return jnp.einsum(mix_form, weights, values, preferred_element_type=jnp.float32).astype(
        jnp.bfloat16
    )


def heads_in(normed_rows, weight_flat):
    return jnp.dot(
        lax.all_gather(normed_rows, "tp", axis=0, tiled=True),
        weight_flat,
        preferred_element_type=jnp.float32,
    )


def heads_out(attended_rows, weight_local):
    return lax.psum_scatter(
        jnp.dot(attended_rows, weight_local, preferred_element_type=jnp.float32).astype(
            jnp.bfloat16
        ),
        "tp",
        scatter_dimension=0,
        tiled=True,
    ).astype(jnp.float32)


def feed_forward(hidden, gains, w_in, w_out):
    model_width = hidden.shape[-1]
    normed = modulate(hidden, gains).reshape(-1, model_width)
    inner = jax.nn.gelu(heads_in(normed, w_in), approximate=True).astype(jnp.bfloat16)
    summed = heads_out(inner, w_out)
    return hidden + gains[2] * summed.reshape(hidden.shape)


def on_device(
    latents, time_embed, modulation, qkv_weight, out_weight, mlp_in_weight, mlp_out_weight
):
    model_width = latents.shape[2]
    local_frames = latents.shape[1]
    local_columns = qkv_weight.shape[3]
    heads_local = local_columns // HD
    flat_spatial = qkv_weight[0].reshape(model_width, 3 * local_columns)
    flat_temporal = qkv_weight[1].reshape(model_width, 3 * local_columns)
    spatial_scores = "pfhd,qfhd->fhpq"
    spatial_mix = "fhpq,qfhd->pfhd"
    temporal_scores = "pfhd,pghd->phfg"
    temporal_mix = "phfg,pghd->pfhd"
    normed = modulate(latents, modulation[0]).reshape(-1, model_width)
    packed = heads_in(normed, flat_spatial).reshape(-1, local_frames, 3, heads_local, HD)
    attended = attend(
        packed[:, :, 0],
        packed[:, :, 1],
        packed[:, :, 2].astype(jnp.bfloat16),
        spatial_scores,
        spatial_mix,
    )
    projected = heads_out(attended.reshape(-1, local_columns), out_weight[0])
    middle = latents + modulation[0, 2] * projected.reshape(latents.shape) + time_embed[None]
    regrouped = lax.all_to_all(middle, "seq", split_axis=0, concat_axis=1, tiled=True)
    all_frames = regrouped.shape[1]
    normed = modulate(regrouped, modulation[1]).reshape(-1, model_width)
    packed = heads_in(normed, flat_temporal).reshape(-1, all_frames, 3, heads_local, HD)
    attended = attend(
        packed[:, :, 0],
        packed[:, :, 1],
        packed[:, :, 2].astype(jnp.bfloat16),
        temporal_scores,
        temporal_mix,
    )
    projected = heads_out(attended.reshape(-1, local_columns), out_weight[1])
    after_t = regrouped + modulation[1, 2] * projected.reshape(regrouped.shape)
    output = feed_forward(after_t, modulation[2], mlp_in_weight, mlp_out_weight)
    return lax.all_to_all(output, "seq", split_axis=1, concat_axis=0, tiled=True)


def solution(mesh):
    in_specs = (
        P("tp", "seq", None),
        P("seq", None),
        P(),
        P(None, None, None, "tp"),
        P(None, "tp", None),
        P(None, "tp"),
        P("tp", None),
    )
    out_specs = P("tp", "seq", None)
    return jax.shard_map(
        on_device, mesh=mesh, in_specs=in_specs, out_specs=out_specs, check_vma=False
    )
```

profile of v0, /device:TPU:1, one launch (start us, length us, event | category | flops | bytes accessed | tf_op | source)
XLA Modules:
  0.0 478.0 jit_solution(6980309448226441714)
XLA Ops:
  6.5 1.7 reduce_sum.72
  8.2 1.8 multiply_reduce_fusion.4
  10.1 0.1 slice_reduce_fusion.1
  10.2 0.5 add_convert_fusion.2
  10.7 1.0 reshape.195
  11.7 4.4 fusion.48
  16.2 46.0 %all-gather.4.cloned.1.call-done = bf16[1024,1152]{1,0:T(8,128)(2,1)} async-done(((bf16[256,1152]{1,0:T(8,128)(2,1)}), bf16[1024,1152]{1,0:T(8,128)(2,1)}) %all-gather.4.cloned.1.call-update) | async-done | bytes 2359312 | tf_op jit(solution)/shard_map/all_gather | solution.py:32
  62.2 5.1 %dot_general.42 = bf16[256,4,1152]{2,1,0:T(4,128)(2,1)} reshape(bf16[1024,1152]{1,0:T(8,128)(2,1)} %all-gather.4.cloned.1.call-done) | data formatting | bytes 4718592 | tf_op jit(solution)/shard_map/dot_general | solution.py:31
  67.3 4.7 fusion.17
  72.1 3.5 fusion.32
  75.6 3.2 fusion.49
  78.9 0.5 fusion.29
  79.4 1.7 copy.17
  81.1 2.0 reshape.196
  83.1 3.9 convolution_convert_fusion.1
  87.1 56.4 %reduce-scatter.4.cloned.1.call-done = bf16[256,1152]{1,0:T(8,128)(2,1)} async-done(((bf16[1024,1152]{1,0:T(8,128)(2,1)}), bf16[256,1152]{1,0:T(8,128)(2,1)}) %reduce-scatter.4.cloned.1.call-update) | async-done | bytes 589840 | tf_op jit(solution)/shard_map/reduce_scatter | solution.py:39
  143.5 2.4 reshape.201
  146.0 1.9 add_add_fusion
  147.9 38.5 %all_to_all.24 = f32[64,4,1152]{2,1,0:T(4,128)} all-to-all(f32[64,4,1152]{2,1,0:T(4,128)S(1)} %add_add_fusion), channel_id=1, replica_groups=mesh['seq'=64,'tp'=4] {'seq'}, dimensions={0} | all-to-all | bytes 2359296 | tf_op jit(solution)/shard_map/all_to_all | solution.py:81
  186.4 1.5 reduce_sum.75
  187.9 0.1 div.41
  188.0 1.7 multiply_reduce_fusion.3
  189.7 0.1 rsqrt.29
  189.8 2.6 all_to_all.9
  192.5 2.4 add_convert_fusion.1
  194.9 41.6 %all-gather.6.cloned.1.call-done = bf16[1024,1152]{1,0:T(8,128)(2,1)} async-done(((bf16[256,1152]{1,0:T(8,128)(2,1)}), bf16[1024,1152]{1,0:T(8,128)(2,1)}) %all-gather.6.cloned.1.call-update) | async-done | bytes 2359312 | tf_op jit(solution)/shard_map/all_gather | solution.py:32
  236.6 4.8 fusion.53
  241.3 3.5 fusion.31
  244.8 3.2 fusion.50
  248.1 0.5 fusion.30
  248.6 0.5 copy.19
  249.1 0.1 copy.28
  249.2 0.7 copy-done.6
  249.9 2.9 convolution_convert_fusion
  252.9 56.4 %reduce-scatter.6.cloned.1.call-done = bf16[256,1152]{1,0:T(8,128)(2,1)} async-done(((bf16[1024,1152]{1,0:T(8,128)(2,1)}), bf16[256,1152]{1,0:T(8,128)(2,1)}) %reduce-scatter.6.cloned.1.call-update) | async-done | bytes 589840 | tf_op jit(solution)/shard_map/reduce_scatter | solution.py:39
  309.3 1.8 fusion.47
  311.1 0.1 copy-done.3
  311.2 0.3 multiply_reduce_fusion.2
  311.6 1.1 add_convert_fusion
  312.8 0.3 reduce-scatter.8.cloned.1.call-start
  313.0 42.6 %all-gather.8.cloned.1.call-done = bf16[1024,1152]{1,0:T(8,128)(2,1)} async-done(((bf16[256,1152]{1,0:T(8,128)(2,1)}), bf16[1024,1152]{1,0:T(8,128)(2,1)}) %all-gather.8.cloned.1.call-update) | async-done | bytes 2359312 | tf_op jit(solution)/shard_map/all_gather | solution.py:32
  355.7 10.1 %convolution_convert_fusion.2 = bf16[1024,1152]{1,0:T(8,128)(2,1)} fusion(bf16[1152,1152]{1,0:T(8,128)(2,1)S(1)} %copy-done, bf16[1024,1152]{1,0:T(8,128)(2,1)} %all-gather.8.cloned.1.call-done, bf16[1152,1152]{1,0:T(8,128)(2,1)} %param.12), kind=kOutput, calls=%fused_computation.17 | convolution fusion | flops 5447614464 | bytes 10027008 | tf_op jit(solution)/shard_map/dot_general | solution.py:40
  365.8 56.4 %reduce-scatter.8.cloned.1.call-done = bf16[256,1152]{1,0:T(8,128)(2,1)} async-done(((bf16[1024,1152]{1,0:T(8,128)(2,1)}), bf16[256,1152]{1,0:T(8,128)(2,1)}) %reduce-scatter.8.cloned.1.call-update) | async-done | bytes 589840 | tf_op jit(solution)/shard_map/reduce_scatter | solution.py:39
  422.3 1.7 add_bitcast_fusion
  424.0 1.2 copy.20
  425.2 38.3 %all_to_all.25 = f32[1,256,1152]{2,0,1:T(1,128)} all-to-all(f32[1,256,1152]{2,0,1:T(1,128)S(1)} %copy.20), channel_id=1, replica_groups=mesh['seq'=64,'tp'=4] {'seq'}, dimensions={1} | all-to-all | bytes 2359296 | tf_op jit(solution)/shard_map/all_to_all | solution.py:95
  463.5 5.1 %reduce.16 = f32[256,1152]{1,0:T(8,128)} reduce(f32[1,256,1152]{2,0,1:T(1,128)} %all_to_all.25, f32[]{:T(128)} %constant.29), dimensions={0}, to_apply=%all_to_all.20.reduce_sub_computation | reduce | bytes 2359300 | tf_op jit(solution)/shard_map/all_to_all | solution.py:95
  468.6 2.6 all_to_all.21
  (29 shorter events, 0.3 us)
Async XLA Ops:
  6.5 349.1 %copy-start = (bf16[1152,1152]{1,0:T(8,128)(2,1)S(1)}, bf16[1152,1152]{1,0:T(8,128)(2,1)}, u32[]{:S(2)}) copy-start(bf16[1152,1152]{1,0:T(8,128)(2,1)} %param.13) | copy-start | bytes 7962628
  6.5 3.5 copy-start.4
  6.5 55.7 %all-gather.4.cloned.1.call-start = ((), (), s32[]{:S(2)}) async-start(), calls=%async_computation.5 | async-start | bytes 2949120 | tf_op jit(solution)/shard_map/all_gather | solution.py:32
  8.2 2.0 copy-start.2
  11.7 131.8 %reduce-scatter.4.cloned.1.call-start = ((), (), s32[]{:S(2)}) async-start(), calls=%async_computation.6 | async-start | bytes 2949120 | tf_op jit(solution)/shard_map/reduce_scatter | solution.py:39
  87.1 58.9 %copy-start.5 = (f32[4,1152]{1,0:T(4,128)S(1)}, f32[4,1152]{1,0:T(4,128)}, u32[]{:S(2)}) copy-start(f32[4,1152]{1,0:T(4,128)} %param.8) | copy-start | bytes 55300
  87.1 149.5 %all-gather.6.cloned.1.call-start = ((), (), s32[]{:S(2)}) async-start(), calls=%async_computation.7 | async-start | bytes 2949120 | tf_op jit(solution)/shard_map/all_gather | solution.py:32
  194.9 114.4 %reduce-scatter.6.cloned.1.call-start = ((), (), s32[]{:S(2)}) async-start(), calls=%async_computation.8 | async-start | bytes 2949120 | tf_op jit(solution)/shard_map/reduce_scatter | solution.py:39
  248.6 1.3 copy-start.6
  252.9 102.8 %all-gather.8.cloned.1.call-start = ((), (), s32[]{:S(2)}) async-start(), calls=%async_computation.9 | async-start | bytes 2949120 | tf_op jit(solution)/shard_map/all_gather | solution.py:32
  309.3 1.8 copy-start.1
  309.3 1.9 copy-start.3
  312.8 109.5 %reduce-scatter.8.cloned.1.call-start = ((), (), s32[]{:S(2)}) async-start(), calls=%async_computation.10 | async-start | bytes 2949120 | tf_op jit(solution)/shard_map/reduce_scatter | solution.py:39
Sparse Core Ops, SparseCore 0:
  11.8 50.3 all-gather.3
  87.2 56.2 reduce-scatter.3
  195.0 41.5 all-gather.5
  253.0 56.2 reduce-scatter.5
  312.9 42.7 all-gather.7
  366.0 56.2 reduce-scatter.7
where the time goes:
time: 479 us; the launch traced here: 478 us
  waiting for transfers between devices  300 us (63%)
  blocking collectives  76.8 us (16%)
  matrix products  34.6 us (7%)
  other arithmetic  28.2 us (6%)
  local copies, waits for them, and re-layouts  24.8 us (5%)
  between operations  13.7 us (3%)
    reduce_scatter x3, waiting for transfers between devices, heads_out(): lax.psum_scatter(jnp.dot(attended_rows, weight_local, preferred_element_t...  169 us
    all_gather x3, waiting for transfers between devices, heads_in(): lax.all_gather(normed_rows, 'tp', axis=0, tiled=True)  130 us
    all_to_all x1, blocking collectives, on_device(): lax.all_to_all(middle, 'seq', split_axis=0, concat_axis=1, tiled=True)  38.5 us
    all_to_all x1, blocking collectives, on_device(): lax.all_to_all(output, 'seq', split_axis=1, concat_axis=0, tiled=True)  38.3 us
    dot_general x3, matrix products, heads_out(): jnp.dot(attended_rows, weight_local, preferred_element_type=jnp.float32)  17 us
  transfers between devices with their start and end apart: 6, of which 6 were waited for; matrix products, arithmetic and copies ran while one was open for 1% of the time, Pallas kernels for 0%

commit v1 on v0

v1 whole, which is shorter than its diff:
```python
import math

import jax
import jax.numpy as jnp
from jax import lax
from jax.experimental import pallas as pl
from jax.experimental.pallas import tpu as pltpu
from jax.sharding import PartitionSpec as P

HD = 72
BF = jnp.bfloat16
F32 = jnp.float32
PLANE = [[x * 16 + z * 4 + y for x in range(4) for y in range(4)] for z in range(4)]
SWAPS = {d: [(t, t ^ d) for t in range(4)] for d in (1, 2, 3)}


def modulate(hidden, gains):
    average = jnp.mean(hidden, axis=-1, keepdims=True)
    centred = hidden - average
    spread = jnp.mean(centred * centred, axis=-1, keepdims=True)
    return (centred * lax.rsqrt(spread + 1e-06) * (1.0 + gains[1]) + gains[0]).astype(BF)


def dot(a, b, ca, cb):
    return lax.dot_general(a, b, (((ca,), (cb,)), ((), ())), preferred_element_type=F32)


def attend_kernel(x_ref, w0, w1, w2, w3, out_ref, held, sems):
    sources = (w0, w1, w2, w3)
    heads = 4
    width = heads * HD
    for k in range(4):
        pltpu.make_async_copy(sources[k], held.at[k], sems.at[k]).start()
    x = x_ref[...]

    def shard(k):
        pltpu.make_async_copy(sources[k], held.at[k], sems.at[k]).wait()
        packed = dot(held[k, : 3 * width, :], x, 1, 1)
        mixed = []
        for h in range(heads):
            q = packed[h * HD : (h + 1) * HD] * (math.log2(math.e) / math.sqrt(HD))
            kk = packed[width + h * HD : width + (h + 1) * HD]
            v = packed[2 * width + h * HD : 2 * width + (h + 1) * HD].astype(BF)
            qh = q.astype(BF).astype(F32)
            kh = kk.astype(BF).astype(F32)
            left = jnp.concatenate([kh, kh, kk - kh], axis=0).astype(BF)
            right = jnp.concatenate([qh, q - qh, qh], axis=0).astype(BF)
            scores = dot(left, right, 0, 0)
            top = jnp.max(scores, axis=0, keepdims=True)
            weights = jnp.exp2(scores - top)
            total = jnp.sum(weights, axis=0, keepdims=True)
            mixed.append(dot(v, weights.astype(BF), 1, 0) / total)
        rows = jnp.concatenate(mixed, axis=0).astype(BF)
        return dot(rows, held[k, 3 * width :, :], 0, 0)

    total = shard(0)
    for k in range(1, 4):
        total = total + shard(k)
    out_ref[...] = total.astype(out_ref.dtype)


def attend(x, shards):
    rows, width = x.shape
    return pl.pallas_call(
        attend_kernel,
        out_shape=jax.ShapeDtypeStruct((rows, width), BF),
        in_specs=[pl.BlockSpec(memory_space=pltpu.VMEM)] + [pl.BlockSpec(memory_space=pl.ANY)] * 4,
        out_specs=pl.BlockSpec(memory_space=pltpu.VMEM),
        scratch_shapes=[
            pltpu.VMEM((4, width, width), BF),
            pltpu.SemaphoreType.DMA((4,)),
        ],
        compiler_params=pltpu.CompilerParams(vmem_limit_bytes=48 * 2**20),
        cost_estimate=pl.CostEstimate(
            flops=2 * rows * width * width * 4, bytes_accessed=8 * width * width, transcendentals=0
        ),
    )(x, *shards)


def mlp_kernel(x_ref, a0, a1, a2, a3, b0, b1, b2, b3, out_ref, held, sems):
    sources = (a0, b0, a1, b1, a2, b2, a3, b3)
    for k in range(8):
        pltpu.make_async_copy(sources[k], held.at[k], sems.at[k]).start()
    x = x_ref[...]
    total = None
    for k in range(4):
        pltpu.make_async_copy(sources[2 * k], held.at[2 * k], sems.at[2 * k]).wait()
        v = dot(x, held[2 * k], 1, 0)
        inner = 0.5 * v * (1.0 + jnp.tanh(math.sqrt(2.0 / math.pi) * (v + 0.044715 * (v * v * v))))
        pltpu.make_async_copy(sources[2 * k + 1], held.at[2 * k + 1], sems.at[2 * k + 1]).wait()
        part = dot(inner.astype(BF), held[2 * k + 1], 1, 0)
        total = part if total is None else total + part
    out_ref[...] = total


def mlp(x, w_in, w_out):
    rows, width = x.shape
    return pl.pallas_call(
        mlp_kernel,
        out_shape=jax.ShapeDtypeStruct((rows, width), F32),
        in_specs=[pl.BlockSpec(memory_space=pltpu.VMEM)] + [pl.BlockSpec(memory_space=pl.ANY)] * 8,
        out_specs=pl.BlockSpec(memory_space=pltpu.VMEM),
        scratch_shapes=[
            pltpu.VMEM((8, width, width), BF),
            pltpu.SemaphoreType.DMA((8,)),
        ],
        compiler_params=pltpu.CompilerParams(vmem_limit_bytes=48 * 2**20),
        cost_estimate=pl.CostEstimate(
            flops=2 * rows * width * width * 8, bytes_accessed=16 * width * width, transcendentals=0
        ),
    )(x, *w_in, *w_out)


def all_shards(own, place):
    piece_rows = own.shape[0] // 16
    piece = lax.dynamic_slice_in_dim(own, place * piece_rows, piece_rows, axis=0)
    piece = lax.ppermute(piece, "tp", SWAPS[2])
    far = lax.all_gather(piece, "seq", axis=0, tiled=True, axis_index_groups=PLANE)
    return own, lax.ppermute(own, "tp", SWAPS[1]), far, lax.ppermute(far, "tp", SWAPS[1])


def on_device(
    latents, time_embed, modulation, qkv_weight, out_weight, mlp_in_weight, mlp_out_weight
):
    width = latents.shape[2]
    seq = lax.axis_index("seq")
    tp = lax.axis_index("tp")
    place = (seq // 16) * 4 + seq % 4
    flat = qkv_weight.transpose(0, 2, 3, 1).reshape(2, -1, width)
    layers = [jnp.concatenate([flat[b], out_weight[b]], axis=0) for b in range(2)]
    spatial = all_shards(layers[0], place)
    temporal = all_shards(layers[1], place)
    w_in = all_shards(mlp_in_weight, place)
    w_out = all_shards(mlp_out_weight, place)

    normed = modulate(latents, modulation[0]).transpose(1, 0, 2)

    def frame(rows, d):
        return lax.dynamic_index_in_dim(rows, tp ^ d, axis=0, keepdims=False)

    parts = [frame(normed, 0)] + [lax.ppermute(frame(normed, d), "tp", SWAPS[d]) for d in (1, 2, 3)]
    projected = attend(jnp.concatenate(parts, axis=0), spatial).reshape(4, -1, width)
    back = [projected[0]] + [lax.ppermute(projected[d], "tp", SWAPS[d]) for d in (1, 2, 3)]
    odd = (tp & 1) == 1
    high = (tp & 2) == 2
    back = [jnp.where(odd, back[d ^ 1], back[d]) for d in range(4)]
    back = [jnp.where(high, back[d ^ 2], back[d]) for d in range(4)]
    projected = jnp.stack(back, axis=1).astype(F32)
    middle = latents + modulation[0, 2] * projected + time_embed[None]
    normed = modulate(middle, modulation[1])
    regrouped = lax.all_to_all(normed, "seq", split_axis=0, concat_axis=0, tiled=True)
    projected = attend(regrouped.reshape(-1, width), temporal).reshape(regrouped.shape)
    projected = lax.all_to_all(projected, "seq", split_axis=0, concat_axis=0, tiled=True)
    after_t = middle + modulation[1, 2] * projected.astype(F32)
    normed = modulate(after_t, modulation[2]).reshape(-1, width)
    projected = mlp(normed, w_in, w_out).reshape(after_t.shape)
    return after_t + modulation[2, 2] * projected


def solution(mesh):
    in_specs = (
        P("tp", "seq", None),
        P("seq", None),
        P(),
        P(None, None, None, "tp"),
        P(None, "tp", None),
        P(None, "tp"),
        P("tp", None),
    )
    out_specs = P("tp", "seq", None)
    return jax.shard_map(
        on_device, mesh=mesh, in_specs=in_specs, out_specs=out_specs, check_vma=False
    )
```

time: 479 us -> 315 us (0.66); the launches traced: 478 us -> 309 us
  waiting for transfers between devices: 300 us -> 134 us
  starting transfers between devices: 0.43 us -> 65.3 us
  blocking collectives: 76.8 us -> 27.5 us
  matrix products: 34.6 us -> 0 us
  Pallas kernels: 0 us -> 34.1 us
  other arithmetic: 28.2 us -> 12.4 us
    reduce_scatter x3 -> x0, waiting for transfers between devices: 169 us -> none  [heads_out(): lax.psum_scatter(jnp.dot(attended_rows, weight_local, preferred_element_t...]
    ppermute x0 -> x18, starting transfers between devices: none -> 51.9 us  [the longest x4 23.2 us: all_shards(): piece = lax.ppermute(piece, 'tp', SWAPS[2])]
    all_to_all x2 -> x1, blocking collectives: 76.8 us -> 27.5 us  [on_device(): lax.all_to_all(projected, 'seq', split_axis=0, concat_axis=0, tiled=True)]
    dot_general x9 -> x0, matrix products: 34.6 us -> none  [the longest x3 17 us: heads_out(): jnp.dot(attended_rows, weight_local, preferred_element_type=jnp.float32)]
    pallas_call x0 -> x3, Pallas kernels: none -> 34.1 us  [the longest x2 24.2 us: attend(): pl.pallas_call(attend_kernel, out_shape=jax.ShapeDtypeStruct((rows, width...]
    ppermute x0 -> x18, waiting for transfers between devices: none -> 33.2 us  [the longest x4 13.5 us: all_shards(): piece = lax.ppermute(piece, 'tp', SWAPS[2])]
    all_gather x3 -> x4, waiting for transfers between devices: 130 us -> 101 us  [all_shards(): lax.all_gather(piece, 'seq', axis=0, tiled=True, axis_index_groups=PLANE)]
    all_to_all x0 -> x1, starting transfers between devices: none -> 13.2 us  [on_device(): lax.all_to_all(normed, 'seq', split_axis=0, concat_axis=0, tiled=True)]
  transfers between devices with their start and end apart: 6 -> 23, of which waited for: 6 -> 11; matrix products, arithmetic and copies ran while one was open for 1% -> 6% of each run, Pallas kernels for 0% -> 8%
where the time goes in v1:
time: 315 us; the launch traced here: 309 us
  waiting for transfers between devices  134 us (43%)
  starting transfers between devices  65.3 us (21%)
  Pallas kernels  34.1 us (11%)
  blocking collectives  27.5 us (9%)
  local copies, waits for them, and re-layouts  21.5 us (7%)
  between operations  13.9 us (4%)
  other arithmetic  12.4 us (4%)
    all_gather x4, waiting for transfers between devices, all_shards(): lax.all_gather(piece, 'seq', axis=0, tiled=True, axis_index_groups=PLANE)  101 us
    all_to_all x1, blocking collectives, on_device(): lax.all_to_all(projected, 'seq', split_axis=0, concat_axis=0, tiled=True)  27.5 us
    pallas_call x2, Pallas kernels, attend(): pl.pallas_call(attend_kernel, out_shape=jax.ShapeDtypeStruct((rows, width...  24.2 us
    ppermute x4, starting transfers between devices, all_shards(): piece = lax.ppermute(piece, 'tp', SWAPS[2])  23.2 us
    ppermute x4, waiting for transfers between devices, all_shards(): piece = lax.ppermute(piece, 'tp', SWAPS[2])  13.5 us
    all_to_all x1, starting transfers between devices, on_device(): lax.all_to_all(normed, 'seq', split_axis=0, concat_axis=0, tiled=True)  13.2 us
    ppermute x3, waiting for transfers between devices, on_device(): lax.ppermute(frame(normed, d), 'tp', SWAPS[d])  12.6 us
    ppermute x3, starting transfers between devices, on_device(): lax.ppermute(frame(normed, d), 'tp', SWAPS[d])  9.94 us
  transfers between devices with their start and end apart: 23, of which 11 were waited for; matrix products, arithmetic and copies ran while one was open for 6% of the time, Pallas kernels for 8%

profile of v1, /device:TPU:1, one launch (start us, length us, event | category | flops | bytes accessed | tf_op | source)
XLA Modules:
  0.0 309.1 jit_solution(7122329572528856110)
XLA Ops:
  6.5 3.9 %fusion.5 = (bf16[1,3,288,1152]{3,2,1,0:T(8,128)(2,1)S(1)}, bf16[1,3,288,1152]{3,2,1,0:T(8,128)(2,1)}) fusion(bf16[2,3,288,1152]{3,2,1,0:T(8,128)(2,1)} %bitcast.27), kind=kLoop, calls=%fused_computation.53 | loop fusion | bytes 7962624 | tf_op jit(solution)/shard_map/slice | solution.py:130
  10.5 1.2 fusion.2
  11.8 7.8 %collective-permute-start.4 = (bf16[72,1152]{1,0:T(8,128)(2,1)S(1)}, bf16[72,1152]{1,0:T(8,128)(2,1)S(1)}, u32[]{:S(2)}, u32[]{:S(2)}) collective-permute-start(bf16[72,1152]{1,0:T(8,128)(2,1)S(1)} %fusion.2), channel_id=1, source_target_pairs={{0,2},{1,3},{2,0},{3,1},{4,6},{5,7},{6,4},{7,5},{8,10},{9,11},{10,... | collective-permute-start | bytes 497672 | tf_op jit(solution)/shard_map/ppermute | solution.py:117
  19.6 3.4 %collective-permute-done.4 = bf16[72,1152]{1,0:T(8,128)(2,1)S(1)} collective-permute-done((bf16[72,1152]{1,0:T(8,128)(2,1)S(1)}, bf16[72,1152]{1,0:T(8,128)(2,1)S(1)}, u32[]{:S(2)}, u32[]{:S(2)}) %collective-permute-start.4) | collective-permute-done | bytes 165920 | tf_op jit(solution)/shard_map/ppermute | solution.py:117
  23.0 0.7 copy-done.14
  23.9 5.7 %collective-permute-start.10 = (bf16[72,1152]{1,0:T(8,128)(2,1)S(1)}, bf16[72,1152]{1,0:T(8,128)(2,1)S(1)}, u32[]{:S(2)}, u32[]{:S(2)}) collective-permute-start(bf16[72,1152]{1,0:T(8,128)(2,1)S(1)} %fusion.1), channel_id=1, source_target_pairs={{0,2},{1,3},{2,0},{3,1},{4,6},{5,7},{6,4},{7,5},{8,10},{9,11},{10,... | collective-permute-start | bytes 497672 | tf_op jit(solution)/shard_map/ppermute | solution.py:117
  29.5 4.0 %collective-permute-done.10 = bf16[72,1152]{1,0:T(8,128)(2,1)S(1)} collective-permute-done((bf16[72,1152]{1,0:T(8,128)(2,1)S(1)}, bf16[72,1152]{1,0:T(8,128)(2,1)S(1)}, u32[]{:S(2)}, u32[]{:S(2)}) %collective-permute-start.10) | collective-permute-done | bytes 165920 | tf_op jit(solution)/shard_map/ppermute | solution.py:117
  34.3 0.9 constant_dynamic-slice_fusion.1
  35.2 4.2 %collective-permute-start.13 = (bf16[72,1152]{1,0:T(8,128)(2,1)S(1)}, bf16[72,1152]{1,0:T(8,128)(2,1)S(1)}, u32[]{:S(2)}, u32[]{:S(2)}) collective-permute-start(bf16[72,1152]{1,0:T(8,128)(2,1)S(1)} %constant_dynamic-slice_fusion.1), channel_id=1, source_target_pairs={{0,2},{1,3},{2,0},{3,1},{4,6},{5,7},{6,4},{7,5},{8,10},{9,11},{10,... | collective-permute-start | bytes 497672 | tf_op jit(solution)/shard_map/ppermute | solution.py:117
  39.4 5.5 %collective-permute-done.13 = bf16[72,1152]{1,0:T(8,128)(2,1)S(1)} collective-permute-done((bf16[72,1152]{1,0:T(8,128)(2,1)S(1)}, bf16[72,1152]{1,0:T(8,128)(2,1)S(1)}, u32[]{:S(2)}, u32[]{:S(2)}) %collective-permute-start.13) | collective-permute-done | bytes 165920 | tf_op jit(solution)/shard_map/ppermute | solution.py:117
  45.7 1.8 pad_maximum_fusion.w0
  47.4 7.7 %collective-permute-start.3 = (bf16[1152,1152]{1,0:T(8,128)(2,1)S(1)}, bf16[1152,1152]{1,0:T(8,128)(2,1)}, u32[]{:S(2)}, u32[]{:S(2)}) collective-permute-start(bf16[1152,1152]{1,0:T(8,128)(2,1)S(1)} %pad_maximum_fusion.w0), channel_id=1, source_target_pairs={{0,1},{1,0},{2,3},{3,2},{4,5},{5,4},{6,7},{7,6},{8,9},{9,8},{10,11... | collective-permute-start | bytes 7962632 | tf_op jit(solution)/shard_map/ppermute | solution.py:119
  55.1 25.4 %all-gather.5.cloned.1.call-done.w2 = bf16[1152,1152]{1,0:T(8,128)(2,1)} async-done(((bf16[72,1152]{1,0:T(8,128)(2,1)}), bf16[1152,1152]{1,0:T(8,128)(2,1)}) %all-gather.5.cloned.1.call-update) | async-done | bytes 2654224 | tf_op jit(solution)/shard_map/all_gather | solution.py:118
  80.6 1.0 collective-permute-start.5
  81.5 1.6 constant_dynamic-slice_fusion
  83.1 5.5 %collective-permute-start.16 = (bf16[72,1152]{1,0:T(8,128)(2,1)}, bf16[72,1152]{1,0:T(8,128)(2,1)S(1)}, u32[]{:S(2)}, u32[]{:S(2)}) collective-permute-start(bf16[72,1152]{1,0:T(8,128)(2,1)} %constant_dynamic-slice_fusion), channel_id=1, source_target_pairs={{0,2},{1,3},{2,0},{3,1},{4,6},{5,7},{6,4},{7,5},{8,10},{9,11},{10,... | collective-permute-start | bytes 497672 | tf_op jit(solution)/shard_map/ppermute | solution.py:117
  88.6 1.5 reduce_sum.54
  90.2 0.7 slice_reduce_fusion.1
  90.9 1.5 multiply_reduce_fusion.2
  94.1 0.9 collective-permute-start
  95.0 8.8 %collective-permute-start.1 = (bf16[64,1152]{1,0:T(8,128)(2,1)S(1)}, bf16[64,1152]{1,0:T(8,128)(2,1)S(1)}, u32[]{:S(2)}, u32[]{:S(2)}) collective-permute-start(bf16[64,1152]{1,0:T(8,128)(2,1)S(1)} %get-tuple-element.29), channel_id=1, source_target_pairs={{0,2},{1,3},{2,0},{3,1},{4,6},{5,7},{6,4},{7,5},{8,10},{9,11},{10,... | collective-permute-start | bytes 442376 | tf_op jit(solution)/shard_map/ppermute | solution.py:141
  104.0 3.9 %collective-permute-done.1 = bf16[64,1152]{1,0:T(8,128)(2,1)S(1)} collective-permute-done((bf16[64,1152]{1,0:T(8,128)(2,1)S(1)}, bf16[64,1152]{1,0:T(8,128)(2,1)S(1)}, u32[]{:S(2)}, u32[]{:S(2)}) %collective-permute-start.1) | collective-permute-done | bytes 147488 | tf_op jit(solution)/shard_map/ppermute | solution.py:141
  107.9 8.7 %collective-permute-done.2 = bf16[64,1152]{1,0:T(8,128)(2,1)S(1)} collective-permute-done((bf16[64,1152]{1,0:T(8,128)(2,1)S(1)}, bf16[64,1152]{1,0:T(8,128)(2,1)S(1)}, u32[]{:S(2)}, u32[]{:S(2)}) %collective-permute-start.2) | collective-permute-done | bytes 147488 | tf_op jit(solution)/shard_map/ppermute | solution.py:141
  116.7 12.1 %shard_map.73 = bf16[256,1152]{1,0:T(8,128)(2,1)S(1)} custom-call(bf16[256,1152]{1,0:T(8,128)(2,1)S(1)} %pad_maximum_fusion.2.x_ref, bf16[1152,1152]{1,0:T(8,128)(2,1)S(1)} %pad_maximum_fusion.w0, bf16[1152,1152]{1,0:T(8,128)(2,1)} %collective-permute-done.3.w1, bf16[1152,1152]{1,0:T(8,128)(2,1)} %all-gather.5.cloned.1.call-done.w2, ...), custom_call_target="tpu_custom_call" | custom-call | flops 2717908992 | bytes 10616832 | tf_op jit(solution)/shard_map/pallas_call | solution.py:64
  128.8 0.7 fusion.6
  129.5 5.5 %collective-permute-start.6 = (bf16[64,1152]{1,0:T(8,128)(2,1)}, bf16[64,1152]{1,0:T(8,128)(2,1)}, u32[]{:S(2)}, u32[]{:S(2)}) collective-permute-start(bf16[64,1152]{1,0:T(8,128)(2,1)} %get-tuple-element.26), channel_id=1, source_target_pairs={{0,3},{1,2},{2,1},{3,0},{4,7},{5,6},{6,5},{7,4},{8,11},{9,10},{10,... | collective-permute-start | bytes 442376 | tf_op jit(solution)/shard_map/ppermute | solution.py:143
  135.0 0.7 collective-permute-start.7
  136.9 3.1 collective-permute-done.6
  139.9 4.0 %collective-permute-done.7 = bf16[64,1152]{1,0:T(8,128)(2,1)} collective-permute-done((bf16[64,1152]{1,0:T(8,128)(2,1)S(1)}, bf16[64,1152]{1,0:T(8,128)(2,1)}, u32[]{:S(2)}, u32[]{:S(2)}) %collective-permute-start.7) | collective-permute-done | bytes 147488 | tf_op jit(solution)/shard_map/ppermute | solution.py:143
  143.9 1.1 select_bitcast_fusion.3
  145.1 1.0 fusion.4
  147.1 1.3 copy.55
  148.4 13.2 %all-to-all-start = ((bf16[64,4,1152]{2,1,0:T(4,128)(2,1)}), bf16[64,4,1152]{2,1,0:T(4,128)(2,1)}, u32[]{:S(2)}, u32[]{:S(2)}) async-start(bf16[64,4,1152]{2,1,0:T(4,128)(2,1)} %copy.55), calls=%async_computation | async-start | bytes 1179648 | tf_op jit(solution)/shard_map/all_to_all | solution.py:151
  161.7 1.0 collective-permute-start.12
  162.8 25.6 %all-gather.9.cloned.1.call-done.a2 = bf16[1152,1152]{1,0:T(8,128)(2,1)} async-done(((bf16[72,1152]{1,0:T(8,128)(2,1)}), bf16[1152,1152]{1,0:T(8,128)(2,1)}) %all-gather.9.cloned.1.call-update) | async-done | bytes 2654224 | tf_op jit(solution)/shard_map/all_gather | solution.py:118
  188.4 0.9 collective-permute-start.14
  189.3 1.5 reshape.83.x_ref
  190.8 50.0 %all-gather.11.cloned.1.call-done.b2 = bf16[1152,1152]{1,0:T(8,128)(2,1)} async-done(((bf16[72,1152]{1,0:T(8,128)(2,1)}), bf16[1152,1152]{1,0:T(8,128)(2,1)}) %all-gather.11.cloned.1.call-update) | async-done | bytes 2654224 | tf_op jit(solution)/shard_map/all_gather | solution.py:118
  240.8 1.0 collective-permute-start.17
  241.8 12.1 %shard_map.74 = bf16[256,1152]{1,0:T(8,128)(2,1)S(1)} custom-call(bf16[256,1152]{1,0:T(8,128)(2,1)S(1)} %reshape.83.x_ref, bf16[1152,1152]{1,0:T(8,128)(2,1)S(1)} %pad_maximum_fusion.1.w0, bf16[1152,1152]{1,0:T(8,128)(2,1)} %collective-permute-done.9.w1, bf16[1152,1152]{1,0:T(8,128)(2,1)} %all-gather.7.cloned.1.call-done.w2, ...), custom_call_target="tpu_custom_call" | custom-call | flops 2717908992 | bytes 10616832 | tf_op jit(solution)/shard_map/pallas_call | solution.py:64
  253.9 0.8 copy-done.1
  254.7 1.6 reshape.84
  256.3 27.5 %all_to_all.10 = bf16[64,4,1152]{2,1,0:T(4,128)(2,1)S(1)} all-to-all(bf16[64,4,1152]{2,1,0:T(4,128)(2,1)S(1)} %reshape.84), channel_id=1, replica_groups=mesh['seq'=64,'tp'=4] {'seq'}, dimensions={0} | all-to-all | bytes 1179648 | tf_op jit(solution)/shard_map/all_to_all | solution.py:153
  285.9 1.7 copy-done
  287.6 9.9 %shard_map.75 = f32[256,1152]{1,0:T(8,128)S(1)} custom-call(bf16[256,1152]{1,0:T(8,128)(2,1)S(1)} %reshape.85.x_ref, bf16[1152,1152]{1,0:T(8,128)(2,1)S(1)} %copy-done, bf16[1152,1152]{1,0:T(8,128)(2,1)} %collective-permute-done.12.a1, bf16[1152,1152]{1,0:T(8,128)(2,1)} %all-gather.9.cloned.1.call-done.a2, bf16[1152,1152]{1,0:T(8,128)(2,1)} %collective-permute-done.14.a3, ...), custom_call_target="tpu_custom_call" | custom-call | flops 5435817984 | bytes 21233664 | tf_op jit(solution)/shard_map/pallas_call | solution.py:98
  297.5 1.4 reshape.86
  298.9 1.5 fusion
  300.4 1.8 copy.59
  (85 shorter events, 7.9 us)
Async XLA Ops:
  6.5 74.0 %all-gather.5.cloned.1.call-start = ((), (), s32[]{:S(2)}) async-start(), calls=%async_computation.2 | async-start | bytes 2820096 | tf_op jit(solution)/shard_map/all_gather | solution.py:118
  6.5 3.9 %copy-start.10 = (bf16[2,288,1152]{2,1,0:T(8,128)(2,1)S(1)}, bf16[2,288,1152]{2,1,0:T(8,128)(2,1)}, u32[]{:S(2)}) copy-start(bf16[2,288,1152]{2,1,0:T(8,128)(2,1)} %param.11) | copy-start | bytes 3981316
  10.4 13.3 %copy-start.6 = (bf16[1,3,288,1152]{3,2,1,0:T(8,128)(2,1)}, bf16[1,3,288,1152]{3,2,1,0:T(8,128)(2,1)S(1)}, u32[]{:S(2)}) copy-start(bf16[1,3,288,1152]{3,2,1,0:T(8,128)(2,1)S(1)} %get-tuple-element.16) | copy-start | bytes 5971972
  10.5 13.2 %copy-start.8 = (bf16[288,1152]{1,0:T(8,128)(2,1)}, bf16[288,1152]{1,0:T(8,128)(2,1)S(1)}, u32[]{:S(2)}) copy-start(bf16[288,1152]{1,0:T(8,128)(2,1)S(1)} %get-tuple-element.18) | copy-start | bytes 1990660
  11.8 11.3 %collective-permute-start.4 = (bf16[72,1152]{1,0:T(8,128)(2,1)S(1)}, bf16[72,1152]{1,0:T(8,128)(2,1)S(1)}, u32[]{:S(2)}, u32[]{:S(2)}) collective-permute-start(bf16[72,1152]{1,0:T(8,128)(2,1)S(1)} %fusion.2), channel_id=1, source_target_pairs={{0,2},{1,3},{2,0},{3,1},{4,6},{5,7},{6,4},{7,5},{8,10},{9,11},{10,... | collective-permute-start | bytes 497672 | tf_op jit(solution)/shard_map/ppermute | solution.py:117
  23.0 0.7 copy-start.14
  23.7 112.8 %all-gather.7.cloned.1.call-start = ((), (), s32[]{:S(2)}) async-start(), calls=%async_computation.3 | async-start | bytes 2820096 | tf_op jit(solution)/shard_map/all_gather | solution.py:118
  23.9 9.7 %collective-permute-start.10 = (bf16[72,1152]{1,0:T(8,128)(2,1)S(1)}, bf16[72,1152]{1,0:T(8,128)(2,1)S(1)}, u32[]{:S(2)}, u32[]{:S(2)}) collective-permute-start(bf16[72,1152]{1,0:T(8,128)(2,1)S(1)} %fusion.1), channel_id=1, source_target_pairs={{0,2},{1,3},{2,0},{3,1},{4,6},{5,7},{6,4},{7,5},{8,10},{9,11},{10,... | collective-permute-start | bytes 497672 | tf_op jit(solution)/shard_map/ppermute | solution.py:117
  33.5 0.7 copy-start.13
  34.2 154.2 %all-gather.9.cloned.1.call-start = ((), (), s32[]{:S(2)}) async-start(), calls=%async_computation.4 | async-start | bytes 2820096 | tf_op jit(solution)/shard_map/all_gather | solution.py:118
  35.2 9.7 %collective-permute-start.13 = (bf16[72,1152]{1,0:T(8,128)(2,1)S(1)}, bf16[72,1152]{1,0:T(8,128)(2,1)S(1)}, u32[]{:S(2)}, u32[]{:S(2)}) collective-permute-start(bf16[72,1152]{1,0:T(8,128)(2,1)S(1)} %constant_dynamic-slice_fusion.1), channel_id=1, source_target_pairs={{0,2},{1,3},{2,0},{3,1},{4,6},{5,7},{6,4},{7,5},{8,10},{9,11},{10,... | collective-permute-start | bytes 497672 | tf_op jit(solution)/shard_map/ppermute | solution.py:117
  44.9 0.7 copy-start.11
  45.6 195.2 %all-gather.11.cloned.1.call-start = ((), (), s32[]{:S(2)}) async-start(), calls=%async_computation.5 | async-start | bytes 2820096 | tf_op jit(solution)/shard_map/all_gather | solution.py:118
  47.4 42.8 %copy-start.20 = (f32[3,3,1152]{2,1,0:T(4,128)S(1)}, f32[3,3,1152]{2,1,0:T(4,128)}, u32[]{:S(2)}) copy-start(f32[3,3,1152]{2,1,0:T(4,128)} %param.9) | copy-start | bytes 124420
  47.4 69.2 %collective-permute-start.3 = (bf16[1152,1152]{1,0:T(8,128)(2,1)S(1)}, bf16[1152,1152]{1,0:T(8,128)(2,1)}, u32[]{:S(2)}, u32[]{:S(2)}) collective-permute-start(bf16[1152,1152]{1,0:T(8,128)(2,1)S(1)} %pad_maximum_fusion.w0), channel_id=1, source_target_pairs={{0,1},{1,0},{2,3},{3,2},{4,5},{5,4},{6,7},{7,6},{8,9},{9,8},{10,11... | collective-permute-start | bytes 7962632 | tf_op jit(solution)/shard_map/ppermute | solution.py:119
  80.6 36.1 %collective-permute-start.5 = (bf16[1152,1152]{1,0:T(8,128)(2,1)}, bf16[1152,1152]{1,0:T(8,128)(2,1)}, u32[]{:S(2)}, u32[]{:S(2)}) collective-permute-start(bf16[1152,1152]{1,0:T(8,128)(2,1)} %all-gather.5.cloned.1.call-done.w2), channel_id=1, source_target_pairs={{0,1},{1,0},{2,3},{3,2},{4,5},{5,4},{6,7},{7,6},{8,9},{9,8},{10,11... | collective-permute-start | bytes 7962632 | tf_op jit(solution)/shard_map/ppermute | solution.py:119
  83.1 10.2 %collective-permute-start.16 = (bf16[72,1152]{1,0:T(8,128)(2,1)}, bf16[72,1152]{1,0:T(8,128)(2,1)S(1)}, u32[]{:S(2)}, u32[]{:S(2)}) collective-permute-start(bf16[72,1152]{1,0:T(8,128)(2,1)} %constant_dynamic-slice_fusion), channel_id=1, source_target_pairs={{0,2},{1,3},{2,0},{3,1},{4,6},{5,7},{6,4},{7,5},{8,10},{9,11},{10,... | collective-permute-start | bytes 497672 | tf_op jit(solution)/shard_map/ppermute | solution.py:117
  90.2 2.3 copy-start.4
  93.3 0.7 copy-start.12
  94.1 9.9 %collective-permute-start = (bf16[64,1152]{1,0:T(8,128)(2,1)S(1)}, bf16[64,1152]{1,0:T(8,128)(2,1)S(1)}, u32[]{:S(2)}, u32[]{:S(2)}) collective-permute-start(bf16[64,1152]{1,0:T(8,128)(2,1)S(1)} %get-tuple-element.30), channel_id=1, source_target_pairs={{0,1},{1,0},{2,3},{3,2},{4,5},{5,4},{6,7},{7,6},{8,9},{9,8},{10,11... | collective-permute-start | bytes 442376 | tf_op jit(solution)/shard_map/ppermute | solution.py:141
  95.0 12.9 %collective-permute-start.1 = (bf16[64,1152]{1,0:T(8,128)(2,1)S(1)}, bf16[64,1152]{1,0:T(8,128)(2,1)S(1)}, u32[]{:S(2)}, u32[]{:S(2)}) collective-permute-start(bf16[64,1152]{1,0:T(8,128)(2,1)S(1)} %get-tuple-element.29), channel_id=1, source_target_pairs={{0,2},{1,3},{2,0},{3,1},{4,6},{5,7},{6,4},{7,5},{8,10},{9,11},{10,... | collective-permute-start | bytes 442376 | tf_op jit(solution)/shard_map/ppermute | solution.py:141
  103.8 12.8 %collective-permute-start.2 = (bf16[64,1152]{1,0:T(8,128)(2,1)S(1)}, bf16[64,1152]{1,0:T(8,128)(2,1)S(1)}, u32[]{:S(2)}, u32[]{:S(2)}) collective-permute-start(bf16[64,1152]{1,0:T(8,128)(2,1)S(1)} %get-tuple-element.28), channel_id=1, source_target_pairs={{0,3},{1,2},{2,1},{3,0},{4,7},{5,6},{6,5},{7,4},{8,11},{9,10},{10,... | collective-permute-start | bytes 442376 | tf_op jit(solution)/shard_map/ppermute | solution.py:141
  116.7 19.4 %copy-start.7 = (bf16[1,3,288,1152]{3,2,1,0:T(8,128)(2,1)S(1)}, bf16[1,3,288,1152]{3,2,1,0:T(8,128)(2,1)}, u32[]{:S(2)}) copy-start(bf16[1,3,288,1152]{3,2,1,0:T(8,128)(2,1)} %copy-done.6) | copy-start | bytes 5971972
  128.8 7.3 %copy-start.9 = (bf16[288,1152]{1,0:T(8,128)(2,1)S(1)}, bf16[288,1152]{1,0:T(8,128)(2,1)}, u32[]{:S(2)}) copy-start(bf16[288,1152]{1,0:T(8,128)(2,1)} %copy-done.8) | copy-start | bytes 1990660
  129.5 10.5 %collective-permute-start.6 = (bf16[64,1152]{1,0:T(8,128)(2,1)}, bf16[64,1152]{1,0:T(8,128)(2,1)}, u32[]{:S(2)}, u32[]{:S(2)}) collective-permute-start(bf16[64,1152]{1,0:T(8,128)(2,1)} %get-tuple-element.26), channel_id=1, source_target_pairs={{0,3},{1,2},{2,1},{3,0},{4,7},{5,6},{6,5},{7,4},{8,11},{9,10},{10,... | collective-permute-start | bytes 442376 | tf_op jit(solution)/shard_map/ppermute | solution.py:143
  135.0 9.0 %collective-permute-start.7 = (bf16[64,1152]{1,0:T(8,128)(2,1)S(1)}, bf16[64,1152]{1,0:T(8,128)(2,1)}, u32[]{:S(2)}, u32[]{:S(2)}) collective-permute-start(bf16[64,1152]{1,0:T(8,128)(2,1)S(1)} %get-tuple-element.25), channel_id=1, source_target_pairs={{0,2},{1,3},{2,0},{3,1},{4,6},{5,7},{6,4},{7,5},{8,10},{9,11},{10,... | collective-permute-start | bytes 442376 | tf_op jit(solution)/shard_map/ppermute | solution.py:143
  135.7 8.3 %collective-permute-start.8 = (bf16[64,1152]{1,0:T(8,128)(2,1)S(1)}, bf16[64,1152]{1,0:T(8,128)(2,1)}, u32[]{:S(2)}, u32[]{:S(2)}) collective-permute-start(bf16[64,1152]{1,0:T(8,128)(2,1)S(1)} %get-tuple-element.24), channel_id=1, source_target_pairs={{0,1},{1,0},{2,3},{3,2},{4,5},{5,4},{6,7},{7,6},{8,9},{9,8},{10,11... | collective-permute-start | bytes 442376 | tf_op jit(solution)/shard_map/ppermute | solution.py:143
  136.3 54.5 %collective-permute-start.9 = (bf16[1152,1152]{1,0:T(8,128)(2,1)S(1)}, bf16[1152,1152]{1,0:T(8,128)(2,1)}, u32[]{:S(2)}, u32[]{:S(2)}) collective-permute-start(bf16[1152,1152]{1,0:T(8,128)(2,1)S(1)} %pad_maximum_fusion.1.w0), channel_id=1, source_target_pairs={{0,1},{1,0},{2,3},{3,2},{4,5},{5,4},{6,7},{7,6},{8,9},{9,8},{10,11... | collective-permute-start | bytes 7962632 | tf_op jit(solution)/shard_map/ppermute | solution.py:119
  136.5 8.6 %copy-start.5 = (f32[64,4,1152]{2,1,0:T(4,128)S(1)}, f32[64,4,1152]{2,1,0:T(4,128)}, u32[]{:S(2)}) copy-start(f32[64,4,1152]{2,1,0:T(4,128)} %param.7) | copy-start | bytes 3538948
  136.5 8.6 %copy-start.19 = (f32[1152]{0:T(1024)S(1)}, f32[1152]{0:T(1024)}, u32[]{:S(2)}) copy-start(f32[1152]{0:T(1024)} %get-tuple-element.11) | copy-start | bytes 13828
  136.5 105.3 %collective-permute-start.11 = (bf16[1152,1152]{1,0:T(8,128)(2,1)}, bf16[1152,1152]{1,0:T(8,128)(2,1)}, u32[]{:S(2)}, u32[]{:S(2)}) collective-permute-start(bf16[1152,1152]{1,0:T(8,128)(2,1)} %all-gather.7.cloned.1.call-done.w2), channel_id=1, source_target_pairs={{0,1},{1,0},{2,3},{3,2},{4,5},{5,4},{6,7},{7,6},{8,9},{9,8},{10,11... | collective-permute-start | bytes 7962632 | tf_op jit(solution)/shard_map/ppermute | solution.py:119
  146.1 1.0 copy-start.2
  146.1 0.7 copy-start.17
  146.1 0.8 copy-start.18
  148.4 40.9 %all-to-all-start = ((bf16[64,4,1152]{2,1,0:T(4,128)(2,1)}), bf16[64,4,1152]{2,1,0:T(4,128)(2,1)}, u32[]{:S(2)}, u32[]{:S(2)}) async-start(bf16[64,4,1152]{2,1,0:T(4,128)(2,1)} %copy.55), calls=%async_computation | async-start | bytes 1179648 | tf_op jit(solution)/shard_map/all_to_all | solution.py:151
  161.7 124.1 %collective-permute-start.12 = (bf16[1152,1152]{1,0:T(8,128)(2,1)}, bf16[1152,1152]{1,0:T(8,128)(2,1)}, u32[]{:S(2)}, u32[]{:S(2)}) collective-permute-start(bf16[1152,1152]{1,0:T(8,128)(2,1)} %a0.1), channel_id=1, source_target_pairs={{0,1},{1,0},{2,3},{3,2},{4,5},{5,4},{6,7},{7,6},{8,9},{9,8},{10,11... | collective-permute-start | bytes 7962632 | tf_op jit(solution)/shard_map/ppermute | solution.py:119
  162.7 123.2 %collective-permute-start.15 = (bf16[1152,1152]{1,0:T(8,128)(2,1)}, bf16[1152,1152]{1,0:T(8,128)(2,1)}, u32[]{:S(2)}, u32[]{:S(2)}) collective-permute-start(bf16[1152,1152]{1,0:T(8,128)(2,1)} %b0.1), channel_id=1, source_target_pairs={{0,1},{1,0},{2,3},{3,2},{4,5},{5,4},{6,7},{7,6},{8,9},{9,8},{10,11... | collective-permute-start | bytes 7962632 | tf_op jit(solution)/shard_map/ppermute | solution.py:119
  188.4 97.4 %collective-permute-start.14 = (bf16[1152,1152]{1,0:T(8,128)(2,1)}, bf16[1152,1152]{1,0:T(8,128)(2,1)}, u32[]{:S(2)}, u32[]{:S(2)}) collective-permute-start(bf16[1152,1152]{1,0:T(8,128)(2,1)} %all-gather.9.cloned.1.call-done.a2), channel_id=1, source_target_pairs={{0,1},{1,0},{2,3},{3,2},{4,5},{5,4},{6,7},{7,6},{8,9},{9,8},{10,11... | collective-permute-start | bytes 7962632 | tf_op jit(solution)/shard_map/ppermute | solution.py:119
  240.8 45.0 %collective-permute-start.17 = (bf16[1152,1152]{1,0:T(8,128)(2,1)}, bf16[1152,1152]{1,0:T(8,128)(2,1)}, u32[]{:S(2)}, u32[]{:S(2)}) collective-permute-start(bf16[1152,1152]{1,0:T(8,128)(2,1)} %all-gather.11.cloned.1.call-done.b2), channel_id=1, source_target_pairs={{0,1},{1,0},{2,3},{3,2},{4,5},{5,4},{6,7},{7,6},{8,9},{9,8},{10,11... | collective-permute-start | bytes 7962632 | tf_op jit(solution)/shard_map/ppermute | solution.py:119
  253.9 0.8 copy-start.1
  254.7 29.2 %copy-start.3 = (f32[64,4,1152]{2,0,1:T(8,128)S(1)}, f32[64,4,1152]{2,0,1:T(8,128)}, u32[]{:S(2)}) copy-start(f32[64,4,1152]{2,0,1:T(8,128)} %copy-done.2) | copy-start | bytes 3538948
  284.1 0.7 copy-start.15
  284.1 0.7 copy-start.16
  285.8 1.8 copy-start
Sparse Core Ops, SparseCore 0:
  23.8 56.6 all-gather.4
  83.0 50.7 all-gather.6
  136.3 52.0 all-gather.8
  190.7 50.0 all-gather.10
